TPU v7x, 512 devices: a whole 4x8x8 slice. The times are simulated.
512 devices in a mesh: ctx: 32 (over y_hi, z, core), tp: 16 (over y_lo, x).
Axes of the slice: x: 4, y: 8 (y_hi: 2, y_lo: 4; y = y_hi * 4 + y_lo), z: 8, core: 2. Of those that a mesh axis runs over, the one named last changes fastest.
Arguments:
- queries: bfloat16 [4096, 8192], P('ctx', 'tp'), may hold values from -6 to 6
- keys_in: bfloat16 [4096, 8192], P('ctx', 'tp'), may hold values from -6 to 6
- values_in: bfloat16 [4096, 8192], P('ctx', 'tp'), may hold values from -6 to 6
- decay_rates: float32 [8192, 16], P('tp'), may hold values from 7.324219e-05 to 0.03
- residues: float32 [8192, 16], P('tp'), may hold values from -1.5 to 1.5
- skip_gain: float32 [8192], P('tp'), may hold values from -4 to 4
- cotangent: bfloat16 [4096, 8192], P('ctx', 'tp'), may hold values from -6 to 6
Outputs:
- operator_out: bfloat16 [4096, 8192], P('ctx', 'tp')
- grad_queries: bfloat16 [4096, 8192], P('ctx', 'tp')
- grad_keys: bfloat16 [4096, 8192], P('ctx', 'tp')
- grad_values: bfloat16 [4096, 8192], P('ctx', 'tp')
- grad_residues: float32 [8192, 16], P('tp')
All inputs are finite; a program needn't handle non-finite values.
Results may differ from a plain program's by a relative error of at most 0.0054.
Values may be sent and summed in bfloat16 or wider, within the bound.
A program may use at most 64 MiB of HBM per device.

v0:
```python
from functools import partial
import math
import jax
import jax.numpy as jnp
from jax import lax
from jax.sharding import PartitionSpec as P

D = 8192
ORDER = 16
PRECISE = lax.Precision.HIGHEST


def chain_link(earlier_pair, later_pair):
    return (earlier_pair[0] * later_pair[0], later_pair[0] * earlier_pair[1] + later_pair[1])


def prepare(decay, weight, block_len):
    positions = jnp.arange(block_len + 1, dtype=jnp.float32)
    powers = jnp.exp(-decay[None] * positions[:, None, None])
    unit_scale = jnp.sqrt(1.0 - jnp.exp(-2.0 * decay))
    mode_coef = weight * unit_scale
    short_filter = jnp.einsum("kcn,cn->kc", powers[:block_len], mode_coef, precision=PRECISE)
    lag_table = jnp.arange(block_len)[:, None] - jnp.arange(block_len)[None, :]
    toeplitz = jnp.where((lag_table >= 0)[:, :, None], short_filter[jnp.maximum(lag_table, 0)], 0.0)
    return (positions, powers, unit_scale, mode_coef, toeplitz, lag_table)


def forward_states(in_blocks, powers, decay, carry_in, block_len):
    block_count = in_blocks.shape[0]
    end_states = jnp.einsum("bsc,scn->bcn", in_blocks, powers[:block_len][::-1], precision=PRECISE)
    decays = jnp.broadcast_to(powers[block_len], end_states.shape)
    _, totals = lax.associative_scan(chain_link, (decays, end_states), axis=0)
    distance = block_len * jnp.arange(1, block_count + 1, dtype=jnp.float32)
    states = totals + jnp.exp(-decay[None] * distance[:, None, None]) * carry_in[None]
    before = jnp.concatenate([carry_in[None], states[:-1]], 0)
    return (before, totals[-1])


def backward_states(back_blocks, powers, decay, carry_back, block_len):
    block_count = back_blocks.shape[0]
    start_states = jnp.einsum("btc,tcn->bcn", back_blocks, powers[:block_len], precision=PRECISE)
    decays = jnp.broadcast_to(powers[block_len], start_states.shape)
    _, totals = lax.associative_scan(chain_link, (decays[::-1], start_states[::-1]), axis=0)
    totals = totals[::-1]
    distance = block_len * jnp.arange(block_count, 0, -1, dtype=jnp.float32)
    states = totals + jnp.exp(-decay[None] * distance[:, None, None]) * carry_back[None]
    after = jnp.concatenate([states[1:], carry_back[None]], 0)
    return (after, totals[0])


def forward_work(lines, tables, block_len):
    decay, weight, carry_in = tables
    positions, powers, unit_scale, mode_coef, toeplitz, lag_table = prepare(
        decay, weight, block_len
    )
    in_blocks = lines[0].reshape(-1, block_len, lines[0].shape[1])
    before, _ = forward_states(in_blocks, powers, decay, carry_in, block_len)
    within_block = jnp.einsum("bsc,tsc->btc", in_blocks, toeplitz, precision=PRECISE)
    from_carry = jnp.einsum("bcn,tcn->btc", before, powers[1:] * mode_coef[None], precision=PRECISE)
    return (within_block + from_carry).reshape(lines[0].shape)


def backward_work(lines, tables, block_len):
    decay, weight, carry_in, carry_back = tables
    positions, powers, unit_scale, mode_coef, toeplitz, lag_table = prepare(
        decay, weight, block_len
    )
    in_blocks = lines[0].reshape(-1, block_len, lines[0].shape[1])
    back_blocks = lines[1].reshape(-1, block_len, lines[1].shape[1])
    before, _ = forward_states(in_blocks, powers, decay, carry_in, block_len)
    after, _ = backward_states(back_blocks, powers, decay, carry_back, block_len)
    within_block = jnp.einsum("btc,tsc->bsc", back_blocks, toeplitz, precision=PRECISE)
    from_carry = jnp.einsum(
        "bcn,scn->bsc", after, powers[1:][::-1] * mode_coef[None], precision=PRECISE
    )
    adjoint = (within_block + from_carry).reshape(lines[1].shape)
    carried = jnp.einsum("btc,tcn,bcn->cn", back_blocks, powers[1:], before, precision=PRECISE)
    pairs = jnp.einsum("btc,bsc->tsc", back_blocks, in_blocks, precision=PRECISE)
    pairs = jnp.where((lag_table >= 0)[:, :, None], pairs, 0.0)
    rising = jnp.exp(decay[None] * positions[:block_len, None, None])
    inside = jnp.einsum("tsc,tcn,scn->cn", pairs, powers[:block_len], rising, precision=PRECISE)
    return (adjoint, unit_scale * (carried + inside))


def to_groups(line_array, group_width):
    seq_rows, channels = line_array.shape
    return jnp.moveaxis(line_array.reshape(seq_rows, channels // group_width, group_width), 1, 0)


def from_groups(stacked):
    group_count, seq_rows, group_width = stacked.shape
    return jnp.moveaxis(stacked, 0, 1).reshape(seq_rows, group_count * group_width)


def param_groups(param_table, group_width):
    return param_table.reshape(
        param_table.shape[0] // group_width, group_width, param_table.shape[1]
    )


def grouped(work_fn, lines, tables, group_width):
    stacked_lines = tuple((to_groups(item, group_width) for item in lines))
    stacked_tables = tuple((param_groups(item, group_width) for item in tables))
    return lax.map(lambda packed: work_fn(packed[0], packed[1]), (stacked_lines, stacked_tables))


def flat_table(stacked):
    return stacked.reshape(stacked.shape[0] * stacked.shape[1], stacked.shape[2])


def shards(queries, keys_in, values_in, decay_rates, residues, skip_gain, cotangent):
    seq_rows, channels = queries.shape
    mode_count = decay_rates.shape[1]
    queries_f = queries.astype(jnp.float32)
    keys_f = keys_in.astype(jnp.float32)
    values_f = values_in.astype(jnp.float32)
    cot_f = cotangent.astype(jnp.float32)
    gated = lax.optimization_barrier((keys_f * values_f).astype(jnp.bfloat16))
    pulled = lax.optimization_barrier((cot_f * queries_f).astype(jnp.bfloat16))
    ctx_count = lax.axis_size("ctx")
    piece_width = channels // ctx_count
    offset = lax.axis_index("ctx") * piece_width
    own_rates = lax.dynamic_slice_in_dim(decay_rates, offset, piece_width, 0)
    own_residues = lax.dynamic_slice_in_dim(residues, offset, piece_width, 0)
    block_len = math.gcd(seq_rows * ctx_count, 128)
    group_width = math.gcd(piece_width, 64)
    zero_state = jnp.zeros((piece_width, mode_count), jnp.float32)
    line_in = lax.all_to_all(gated, "ctx", split_axis=1, concat_axis=0, tiled=True).astype(
        jnp.float32
    )
    conv_line = from_groups(
        grouped(
            partial(forward_work, block_len=block_len),
            (line_in,),
            (own_rates, own_residues, zero_state),
            group_width,
        )
    )
    convolved = lax.all_to_all(
        conv_line.astype(jnp.bfloat16), "ctx", split_axis=0, concat_axis=1, tiled=True
    )
    line_back = lax.all_to_all(pulled, "ctx", split_axis=1, concat_axis=0, tiled=True).astype(
        jnp.float32
    )
    adj_line, raw_grad = grouped(
        partial(backward_work, block_len=block_len),
        (line_in, line_back),
        (own_rates, own_residues, zero_state, zero_state),
        group_width,
    )
    adjoint = lax.all_to_all(
        from_groups(adj_line).astype(jnp.bfloat16), "ctx", split_axis=0, concat_axis=1, tiled=True
    )
    own_raw = flat_table(raw_grad)
    mixed = convolved.astype(jnp.float32) + skip_gain[None, :] * gated.astype(jnp.float32)
    operator_out = (queries_f * mixed).astype(jnp.bfloat16)
    grad_queries = (cot_f * mixed).astype(jnp.bfloat16)
    grad_gated = adjoint.astype(jnp.float32) + skip_gain[None, :] * pulled.astype(jnp.float32)
    grad_keys = (grad_gated * values_f).astype(jnp.bfloat16)
    grad_values = (grad_gated * keys_f).astype(jnp.bfloat16)
    raw_all = lax.all_gather(own_raw, "ctx", axis=0, tiled=True)
    grad_square = lax.psum(jnp.sum(raw_all * raw_all), "tp")
    factor = jnp.minimum(1.0, math.sqrt(D * ORDER) / jnp.sqrt(grad_square + 1e-06))
    grad_residues = raw_all * factor
    return (operator_out, grad_queries, grad_keys, grad_values, grad_residues)


def solution(mesh):
    in_specs = (
        P("ctx", "tp"),
        P("ctx", "tp"),
        P("ctx", "tp"),
        P("tp", None),
        P("tp", None),
        P("tp"),
        P("ctx", "tp"),
    )
    out_specs = (P("ctx", "tp"), P("ctx", "tp"), P("ctx", "tp"), P("ctx", "tp"), P("tp", None))
    return jax.shard_map(shards, mesh=mesh, in_specs=in_specs, out_specs=out_specs, check_vma=False)
```

profile of v0, /device:TPU:32, one launch (start us, length us, event | category | flops | bytes accessed | tf_op | source)
XLA Modules:
  0.0 280.1 jit_solution(7708082309188066356)
XLA Ops:
  3.5 15.9 %all-to-all-start = ((bf16[128,32,16]{0,2,1:T(8,128)(2,1)}), bf16[128,32,16]{0,2,1:T(8,128)(2,1)}, u32[]{:S(2)}, u32[]{:S(2)}) async-start(bf16[128,32,16]{0,2,1:T(8,128)(2,1)} %bitcast.8), calls=%async_computation | async-start | bytes 262144 | tf_op jit(solution)/shard_map/all_to_all | solution.py:128
  20.7 1.3 fusion.56
  24.3 54.4 %gather_fusion = f32[16384,16]{1,0:T(8,128)} fusion(f32[128,16]{1,0:T(8,128)S(1)} %bitcast.55, s32[16384]{0:T(1024)S(1)} %bitcast_clamp_fusion), kind=kCustom, calls=%fused_computation | custom fusion | bytes 2162688 | tf_op jit(solution)/shard_map/while/body/eval_jaxpr/gather | solution.py:24
  78.7 6.8 %copy.139 = f32[128,128,16]{0,1,2:T(8,128)S(1)} copy(f32[128,128,16]{2,1,0:T(8,128)} %bitcast.56) | data formatting | bytes 2097152 | tf_op jit(solution)/shard_map/while/body/eval_jaxpr/gather | solution.py:24
  86.2 2.2 fusion.10
  97.1 1.5 fusion.14
  98.6 2.0 fusion.4
  101.4 12.2 %all-to-all-start.1 = ((bf16[32,128,16]{1,2,0:T(8,128)(2,1)}), bf16[32,128,16]{1,2,0:T(8,128)(2,1)S(1)}, u32[]{:S(2)}, u32[]{:S(2)}) async-start(bf16[32,128,16]{1,2,0:T(8,128)(2,1)} %copy.149), calls=%async_computation.1 | async-start | bytes 262144 | tf_op jit(solution)/shard_map/all_to_all | solution.py:139
  115.4 6.9 %all-to-all-done.1 = bf16[32,128,16]{1,2,0:T(8,128)(2,1)S(1)} async-done(((bf16[32,128,16]{1,2,0:T(8,128)(2,1)}), bf16[32,128,16]{1,2,0:T(8,128)(2,1)S(1)}, u32[]{:S(2)}, u32[]{:S(2)}) %all-to-all-start.1) | async-done | bytes 131104 | tf_op jit(solution)/shard_map/all_to_all | solution.py:139
  122.3 1.9 fusion.24
  124.2 8.2 %all-to-all-start.2 = ((bf16[128,32,16]{0,2,1:T(8,128)(2,1)}), bf16[128,32,16]{0,2,1:T(8,128)(2,1)S(1)}, u32[]{:S(2)}, u32[]{:S(2)}) async-start(bf16[128,32,16]{0,2,1:T(8,128)(2,1)} %bitcast.63), calls=%async_computation.2 | async-start | bytes 262144 | tf_op jit(solution)/shard_map/all_to_all | solution.py:142
  134.1 1.7 copy.178
  135.9 1.7 copy.165
  137.6 3.6 %all-to-all-done.2 = bf16[128,32,16]{0,2,1:T(8,128)(2,1)S(1)} async-done(((bf16[128,32,16]{0,2,1:T(8,128)(2,1)}), bf16[128,32,16]{0,2,1:T(8,128)(2,1)S(1)}, u32[]{:S(2)}, u32[]{:S(2)}) %all-to-all-start.2) | async-done | bytes 131104 | tf_op jit(solution)/shard_map/all_to_all | solution.py:142
  142.1 1.7 copy.155
  147.5 1.9 pad.116
  149.4 1.9 pad.117
  151.3 1.4 add.275
  152.7 1.4 fusion.41
  154.1 1.3 slice.495
  155.4 1.4 pad.119
  156.8 1.4 pad_maximum_fusion.5
  158.1 3.2 %pad.118 = f32[8,16,16]{2,1,0:T(8,128)} pad(f32[4,16,16]{2,1,0:T(8,128)} %pad_maximum_fusion.5, f32[]{:T(128)} %constant.76.clone.1), padding=0_1_1x0_0_0x0_0_0 | pad | bytes 12292 | tf_op jit(solution)/shard_map/while/body/eval_jaxpr/pad | solution.py:43
  162.3 1.5 add.277
  163.8 1.6 slice.469
  166.0 1.3 fusion
  167.3 1.8 fusion.6
  169.2 1.1 fusion.5
  170.3 51.1 %all_gather.3 = f32[512,16]{1,0:T(8,128)S(1)} all-gather(f32[16,16]{1,0:T(8,128)S(1)} %add_multiply_fusion.6), channel_id=1, replica_groups=mesh['ctx'=32,'tp'=16] {'ctx'}, dimensions={0}, use_global_device_ids=true | all-gather | bytes 33792 | tf_op jit(solution)/shard_map/all_gather | solution.py:161
  223.6 2.0 fusion.3
  226.3 7.4 %all-to-all-start.3 = ((bf16[32,128,16]{1,2,0:T(8,128)(2,1)}), bf16[32,128,16]{1,2,0:T(8,128)(2,1)S(1)}, u32[]{:S(2)}, u32[]{:S(2)}) async-start(bf16[32,128,16]{1,2,0:T(8,128)(2,1)} %copy.158), calls=%async_computation.3 | async-start | bytes 262144 | tf_op jit(solution)/shard_map/all_to_all | solution.py:151
  235.2 41.7 %psum.7 = f32[]{:T(128)} all-reduce(f32[]{:T(128)} %multiply_reduce_fusion), channel_id=1, replica_groups=mesh['ctx'=32,'tp'=16] {'tp'}, use_global_device_ids=true, to_apply=%region_1.2 | all-reduce | flops 1 | bytes 8 | tf_op jit(solution)/shard_map/psum | solution.py:162
  (146 shorter events, 32.5 us)
Async XLA Ops:
  0.6 18.8 %copy-start = (f32[512,16]{0,1:T(8,128)S(1)}, f32[512,16]{0,1:T(8,128)}, u32[]{:S(2)}) copy-start(f32[512,16]{0,1:T(8,128)} %param.10) | copy-start | bytes 98308
  1.7 19.0 %copy-start.2 = (bf16[128,512]{0,1:T(8,128)(2,1)}, bf16[128,512]{0,1:T(8,128)(2,1)S(1)}, u32[]{:S(2)}) copy-start(bf16[128,512]{0,1:T(8,128)(2,1)S(1)} %copy.140) | copy-start | bytes 393220
  2.8 17.9 %copy-start.4 = (bf16[128,512]{0,1:T(8,128)(2,1)}, bf16[128,512]{0,1:T(8,128)(2,1)S(1)}, u32[]{:S(2)}) copy-start(bf16[128,512]{0,1:T(8,128)(2,1)S(1)} %copy.141) | copy-start | bytes 393220
  3.5 82.7 %all-to-all-start = ((bf16[128,32,16]{0,2,1:T(8,128)(2,1)}), bf16[128,32,16]{0,2,1:T(8,128)(2,1)}, u32[]{:S(2)}, u32[]{:S(2)}) async-start(bf16[128,32,16]{0,2,1:T(8,128)(2,1)} %bitcast.8), calls=%async_computation | async-start | bytes 262144 | tf_op jit(solution)/shard_map/all_to_all | solution.py:128
  19.6 0.9 copy-start.15
  94.1 2.0 copy-start.23
  96.3 2.3 copy-start.1
  98.6 15.0 %copy-start.17 = (bf16[128,512]{1,0:T(8,128)(2,1)S(1)}, bf16[128,512]{1,0:T(8,128)(2,1)}, u32[]{:S(2)}) copy-start(bf16[128,512]{1,0:T(8,128)(2,1)} %param.7) | copy-start | bytes 393220
  98.6 15.8 %copy-start.18 = (bf16[128,512]{1,0:T(8,128)(2,1)S(1)}, bf16[128,512]{1,0:T(8,128)(2,1)}, u32[]{:S(2)}) copy-start(bf16[128,512]{1,0:T(8,128)(2,1)} %param.13) | copy-start | bytes 393220
  98.6 16.6 %copy-start.16 = (f32[16,16]{1,0:T(8,128)S(1)}, f32[16,16]{1,0:T(8,128)}, u32[]{:S(2)}) copy-start(f32[16,16]{1,0:T(8,128)} %copy-done.15) | copy-start | bytes 3076
  100.7 21.6 %copy-start.20 = (f32[512]{0:T(512)S(1)}, f32[512]{0:T(512)}, u32[]{:S(2)}) copy-start(f32[512]{0:T(512)} %param.12) | copy-start | bytes 6148
  101.4 20.9 %all-to-all-start.1 = ((bf16[32,128,16]{1,2,0:T(8,128)(2,1)}), bf16[32,128,16]{1,2,0:T(8,128)(2,1)S(1)}, u32[]{:S(2)}, u32[]{:S(2)}) async-start(bf16[32,128,16]{1,2,0:T(8,128)(2,1)} %copy.149), calls=%async_computation.1 | async-start | bytes 262144 | tf_op jit(solution)/shard_map/all_to_all | solution.py:139
  124.2 16.9 %all-to-all-start.2 = ((bf16[128,32,16]{0,2,1:T(8,128)(2,1)}), bf16[128,32,16]{0,2,1:T(8,128)(2,1)S(1)}, u32[]{:S(2)}, u32[]{:S(2)}) async-start(bf16[128,32,16]{0,2,1:T(8,128)(2,1)} %bitcast.63), calls=%async_computation.2 | async-start | bytes 262144 | tf_op jit(solution)/shard_map/all_to_all | solution.py:142
  144.9 0.7 copy-start.7
  144.9 0.7 copy-start.8
  145.6 0.6 copy-start.13
  161.3 6.0 %copy-start.9 = (f32[16,16,128]{2,1,0:T(8,128)S(1)}, f32[16,16,128]{2,1,0:T(8,128)}, u32[]{:S(2)}) copy-start(f32[16,16,128]{2,1,0:T(8,128)} %copy.184) | copy-start | bytes 393220
  166.0 3.1 %copy-start.10 = (f32[16,16,32]{2,1,0:T(8,128)S(1)}, f32[16,16,32]{2,1,0:T(8,128)}, u32[]{:S(2)}) copy-start(f32[16,16,32]{2,1,0:T(8,128)} %copy.178) | copy-start | bytes 98308
  169.1 52.2 %copy-start.19 = (f32[1,16,16]{2,1,0:T(8,128)S(1)}, f32[1,16,16]{2,1,0:T(8,128)}, u32[]{:S(2)}) copy-start(f32[1,16,16]{2,1,0:T(8,128)} %slice.495) | copy-start | bytes 3076
  169.2 52.3 %copy-start.14 = (f32[8,16,16]{2,1,0:T(8,128)S(1)}, f32[8,16,16]{2,1,0:T(8,128)}, u32[]{:S(2)}) copy-start(f32[8,16,16]{2,1,0:T(8,128)} %add.277) | copy-start | bytes 24580
  170.3 51.4 %copy-start.12 = (f32[15,16,16]{2,1,0:T(8,128)S(1)}, f32[15,16,16]{2,1,0:T(8,128)}, u32[]{:S(2)}) copy-start(f32[15,16,16]{2,1,0:T(8,128)} %slice.469) | copy-start | bytes 46084
  221.8 0.6 copy-start.22
  223.6 10.8 %copy-start.11 = (bf16[128,512]{0,1:T(8,128)(2,1)S(1)}, bf16[128,512]{0,1:T(8,128)(2,1)}, u32[]{:S(2)}) copy-start(bf16[128,512]{0,1:T(8,128)(2,1)} %get-tuple-element.74) | copy-start | bytes 393220
  225.6 52.8 %copy-start.3 = (bf16[128,512]{0,1:T(8,128)(2,1)S(1)}, bf16[128,512]{0,1:T(8,128)(2,1)}, u32[]{:S(2)}) copy-start(bf16[128,512]{0,1:T(8,128)(2,1)} %copy-done.2) | copy-start | bytes 393220
  225.6 52.8 %copy-start.5 = (bf16[128,512]{0,1:T(8,128)(2,1)S(1)}, bf16[128,512]{0,1:T(8,128)(2,1)}, u32[]{:S(2)}) copy-start(bf16[128,512]{0,1:T(8,128)(2,1)} %copy-done.4) | copy-start | bytes 393220
  225.6 52.7 %copy-start.6 = (bf16[128,512]{0,1:T(8,128)(2,1)S(1)}, bf16[128,512]{0,1:T(8,128)(2,1)}, u32[]{:S(2)}) copy-start(bf16[128,512]{0,1:T(8,128)(2,1)} %get-tuple-element.76) | copy-start | bytes 393220
  225.6 52.7 %copy-start.21 = (f32[512]{0:T(512)S(1)}, f32[512]{0:T(512)}, u32[]{:S(2)}) copy-start(f32[512]{0:T(512)} %param.12) | copy-start | bytes 6148
  226.3 52.0 %all-to-all-start.3 = ((bf16[32,128,16]{1,2,0:T(8,128)(2,1)}), bf16[32,128,16]{1,2,0:T(8,128)(2,1)S(1)}, u32[]{:S(2)}, u32[]{:S(2)}) async-start(bf16[32,128,16]{1,2,0:T(8,128)(2,1)} %copy.158), calls=%async_computation.3 | async-start | bytes 262144 | tf_op jit(solution)/shard_map/all_to_all | solution.py:151
where the time goes:
time: 282 us; the launch traced here: 280 us
  local copies, waits for them, and re-layouts  96.8 us (34%)
  blocking collectives  92.8 us (33%)
  starting transfers between devices  43.7 us (15%)
  other arithmetic  20.1 us (7%)
  matrix products  14.2 us (5%)
  waiting for transfers between devices  10.5 us (4%)
    gather x2, local copies, waits for them, and re-layouts, prepare(): short_filter[jnp.maximum(lag_table, 0)]  61.2 us
    all_gather x1, blocking collectives, shards(): raw_all = lax.all_gather(own_raw, 'ctx', axis=0, tiled=True)  51.1 us
    psum x1, blocking collectives, shards(): grad_square = lax.psum(jnp.sum(raw_all * raw_all), 'tp')  41.7 us
    all_to_all x1, starting transfers between devices, shards(): lax.all_to_all(gated, 'ctx', split_axis=1, concat_axis=0, tiled=True)  15.9 us
    unnamed x64, local copies, waits for them, and re-layouts  14 us
    all_to_all x1, starting transfers between devices, shards(): lax.all_to_all(conv_line.astype(jnp.bfloat16), 'ctx', split_axis=0, conca...  12.2 us
    pad x8, local copies, waits for them, and re-layouts, backward_states(): lax.associative_scan(chain_link, (decays[::-1], start_states[::-1]), axis=0)  8.84 us
    all_to_all x1, starting transfers between devices, shards(): lax.all_to_all(pulled, 'ctx', split_axis=1, concat_axis=0, tiled=True)  8.18 us
  transfers between devices with their start and end apart: 4, of which 2 were waited for; matrix products, arithmetic and copies ran while one was open for 27% of the time, Pallas kernels for 0%

commit v1 on v0

--- a/solution.py
+++ b/solution.py
@@ -158,7 +158,10 @@
     grad_gated = adjoint.astype(jnp.float32) + skip_gain[None, :] * pulled.astype(jnp.float32)
     grad_keys = (grad_gated * values_f).astype(jnp.bfloat16)
     grad_values = (grad_gated * keys_f).astype(jnp.bfloat16)
-    raw_all = lax.all_gather(own_raw, "ctx", axis=0, tiled=True)
+    raw_all = jnp.concatenate(
+        jax.lax.all_to_all(jnp.stack(jax.lax.axis_size("ctx") * [own_raw], axis=0), "ctx", 0, 0),
+        axis=0,
+    )
     grad_square = lax.psum(jnp.sum(raw_all * raw_all), "tp")
     factor = jnp.minimum(1.0, math.sqrt(D * ORDER) / jnp.sqrt(grad_square + 1e-06))
     grad_residues = raw_all * factor

time: 282 us -> 299 us (1.060)
  blocking collectives: 92.8 us -> 41.7 us
  local copies, waits for them, and re-layouts: 96.8 us -> 136 us
  other arithmetic: 20.1 us -> 36 us
  starting transfers between devices: 43.7 us -> 57.4 us
    all_gather x1 -> x0, blocking collectives: 51.1 us -> none  [shards(): raw_all = lax.all_gather(own_raw, 'ctx', axis=0, tiled=True)]
    pad x8, local copies, waits for them, and re-layouts: 8.84 us -> 36.5 us  [backward_states(): lax.associative_scan(chain_link, (decays[::-1], start_states[::-1]), axis=0)]
    all_to_all x0 -> x1, starting transfers between devices: none -> 12.1 us  [shards(): jax.lax.all_to_all(jnp.stack(jax.lax.axis_size('ctx') * [own_raw], axis=0...]
    all_to_all x0 -> x1, waiting for transfers between devices: none -> 3.55 us  [shards(): jax.lax.all_to_all(jnp.stack(jax.lax.axis_size('ctx') * [own_raw], axis=0...]
    all_to_all x1, waiting for transfers between devices: 3.57 us -> 0.09 us  [shards(): lax.all_to_all(pulled, 'ctx', split_axis=1, concat_axis=0, tiled=True)]
    add x5, other arithmetic: 3.52 us -> 6.92 us  [backward_states(): lax.associative_scan(chain_link, (decays[::-1], start_states[::-1]), axis=0)]
    unnamed x64 -> x73, local copies, waits for them, and re-layouts: 14 us -> 16.7 us
  transfers between devices with their start and end apart: 4 -> 5, of which waited for: 2 -> 3; matrix products, arithmetic and copies ran while one was open for 27% -> 30% of each run, Pallas kernels for 0% -> 0%
where the time goes in v1:
time: 299 us; the launch traced here: 295 us
  local copies, waits for them, and re-layouts  136 us (45%)
  starting transfers between devices  57.4 us (19%)
  blocking collectives  41.7 us (14%)
  other arithmetic  36 us (12%)
  matrix products  13.6 us (5%)
  waiting for transfers between devices  8.78 us (3%)
    gather x2, local copies, waits for them, and re-layouts, prepare(): short_filter[jnp.maximum(lag_table, 0)]  61.2 us
    psum x1, blocking collectives, shards(): grad_square = lax.psum(jnp.sum(raw_all * raw_all), 'tp')  41.7 us
    pad x8, local copies, waits for them, and re-layouts, backward_states(): lax.associative_scan(chain_link, (decays[::-1], start_states[::-1]), axis=0)  36.5 us
    unnamed x73, local copies, waits for them, and re-layouts  16.7 us
    all_to_all x1, starting transfers between devices, shards(): lax.all_to_all(gated, 'ctx', split_axis=1, concat_axis=0, tiled=True)  15.8 us
    all_to_all x1, starting transfers between devices, shards(): lax.all_to_all(conv_line.astype(jnp.bfloat16), 'ctx', split_axis=0, conca...  12.2 us
    all_to_all x1, starting transfers between devices, shards(): jax.lax.all_to_all(jnp.stack(jax.lax.axis_size('ctx') * [own_raw], axis=0...  12.1 us
    all_to_all x1, starting transfers between devices, shards(): lax.all_to_all(from_groups(adj_line).astype(jnp.bfloat16), 'ctx', split_a...  8.99 us
  transfers between devices with their start and end apart: 5, of which 3 were waited for; matrix products, arithmetic and copies ran while one was open for 30% of the time, Pallas kernels for 0%

profile of v1, /device:TPU:32, one launch (start us, length us, event | category | flops | bytes accessed | tf_op | source)
XLA Modules:
  0.0 295.5 jit_solution(12012188855948047977)
XLA Ops:
  3.5 15.8 %all-to-all-start = ((bf16[128,32,16]{0,2,1:T(8,128)(2,1)}), bf16[128,32,16]{0,2,1:T(8,128)(2,1)S(1)}, u32[]{:S(2)}, u32[]{:S(2)}) async-start(bf16[128,32,16]{0,2,1:T(8,128)(2,1)} %bitcast.6), calls=%async_computation | async-start | bytes 262144 | tf_op jit(solution)/shard_map/all_to_all | solution.py:128
  23.8 54.4 %gather_fusion = f32[16384,16]{1,0:T(8,128)} fusion(f32[128,16]{1,0:T(8,128)S(1)} %bitcast.56, s32[16384]{0:T(1024)S(1)} %bitcast_clamp_fusion), kind=kCustom, calls=%fused_computation | custom fusion | bytes 2162688 | tf_op jit(solution)/shard_map/while/body/eval_jaxpr/gather | solution.py:24
  78.2 6.8 %copy.144 = f32[128,128,16]{0,1,2:T(8,128)S(1)} copy(f32[128,128,16]{2,1,0:T(8,128)} %bitcast.57) | data formatting | bytes 2097152 | tf_op jit(solution)/shard_map/while/body/eval_jaxpr/gather | solution.py:24
  85.1 2.3 rev.18
  88.0 2.3 fusion.10
  99.5 2.0 fusion.4
  102.2 12.2 %all-to-all-start.1 = ((bf16[32,128,16]{1,2,0:T(8,128)(2,1)}), bf16[32,128,16]{1,2,0:T(8,128)(2,1)S(1)}, u32[]{:S(2)}, u32[]{:S(2)}) async-start(bf16[32,128,16]{1,2,0:T(8,128)(2,1)} %copy.156), calls=%async_computation.1 | async-start | bytes 262144 | tf_op jit(solution)/shard_map/all_to_all | solution.py:139
  116.0 2.0 exponential_bitcast_fusion
  118.0 5.1 %all-to-all-done.1 = bf16[32,128,16]{1,2,0:T(8,128)(2,1)S(1)} async-done(((bf16[32,128,16]{1,2,0:T(8,128)(2,1)}), bf16[32,128,16]{1,2,0:T(8,128)(2,1)S(1)}, u32[]{:S(2)}, u32[]{:S(2)}) %all-to-all-start.1) | async-done | bytes 131104 | tf_op jit(solution)/shard_map/all_to_all | solution.py:139
  123.1 1.9 fusion.24
  125.0 8.2 %all-to-all-start.2 = ((bf16[128,32,16]{0,2,1:T(8,128)(2,1)}), bf16[128,32,16]{0,2,1:T(8,128)(2,1)S(1)}, u32[]{:S(2)}, u32[]{:S(2)}) async-start(bf16[128,32,16]{0,2,1:T(8,128)(2,1)} %bitcast.12), calls=%async_computation.2 | async-start | bytes 262144 | tf_op jit(solution)/shard_map/all_to_all | solution.py:142
  135.4 2.3 copy.196
  138.4 1.7 copy.189
  142.9 1.7 copy.162
  149.5 1.9 pad.117
  152.8 1.9 pad.116
  158.2 3.2 %pad.118 = f32[8,16,16]{2,1,0:T(8,128)} pad(f32[4,16,16]{2,1,0:T(8,128)} %pad_maximum_fusion.5, f32[]{:T(128)} %constant.76.clone.1), padding=0_1_1x0_0_0x0_0_0 | pad | bytes 12292 | tf_op jit(solution)/shard_map/while/body/eval_jaxpr/pad | solution.py:43
  161.4 3.2 %pad.119 = f32[8,16,16]{2,1,0:T(8,128)} pad(f32[4,16,16]{2,1,0:T(8,128)} %add.275, f32[]{:T(128)} %constant.76.clone.1), padding=1_0_1x0_0_0x0_0_0 | pad | bytes 12292 | tf_op jit(solution)/shard_map/while/body/eval_jaxpr/pad | solution.py:43
  171.8 4.7 %pad.121 = f32[16,16,16]{2,1,0:T(8,128)} pad(f32[8,16,16]{2,1,0:T(8,128)} %add.277, f32[]{:T(128)} %constant.76.clone.1), padding=1_0_1x0_0_0x0_0_0 | pad | bytes 24580 | tf_op jit(solution)/shard_map/while/body/eval_jaxpr/pad | solution.py:43
  178.0 4.7 %pad.120 = f32[16,16,16]{2,1,0:T(8,128)} pad(f32[8,16,16]{2,1,0:T(8,128)} %pad_maximum_fusion.3, f32[]{:T(128)} %constant.76.clone.1), padding=0_1_1x0_0_0x0_0_0 | pad | bytes 24580 | tf_op jit(solution)/shard_map/while/body/eval_jaxpr/pad | solution.py:43
  186.7 8.4 %pad.122 = f32[32,16,16]{2,1,0:T(8,128)} pad(f32[16,16,16]{2,1,0:T(8,128)} %pad_maximum_fusion.1, f32[]{:T(128)} %constant.76.clone.1), padding=0_1_1x0_0_0x0_0_0 | pad | bytes 49156 | tf_op jit(solution)/shard_map/while/body/eval_jaxpr/pad | solution.py:43
  195.2 8.4 %pad.123 = f32[32,16,16]{2,1,0:T(8,128)} pad(f32[16,16,16]{2,1,0:T(8,128)} %add.279, f32[]{:T(128)} %constant.76.clone.1), padding=1_0_1x0_0_0x0_0_0 | pad | bytes 49156 | tf_op jit(solution)/shard_map/while/body/eval_jaxpr/pad | solution.py:43
  203.6 1.8 add.281
  207.0 1.8 slice_add_fusion
  208.8 1.8 copy.201
  210.6 2.6 fusion.5
  215.4 1.8 fusion.6
  218.2 12.1 %all-to-all-start.4 = ((f32[32,1,256]{2,1,0:T(1,128)}), f32[32,1,256]{2,1,0:T(1,128)S(1)}, u32[]{:S(2)}, u32[]{:S(2)}) async-start(f32[32,1,256]{2,1,0:T(1,128)} %reshape.133), calls=%async_computation.4 | async-start | bytes 65536 | tf_op jit(solution)/shard_map/all_to_all | solution.py:162
  231.2 2.0 fusion.3
  233.9 3.5 %all-to-all-done.4 = f32[32,1,256]{2,1,0:T(1,128)S(1)} async-done(((f32[32,1,256]{2,1,0:T(1,128)}), f32[32,1,256]{2,1,0:T(1,128)S(1)}, u32[]{:S(2)}, u32[]{:S(2)}) %all-to-all-start.4) | async-done | bytes 32800 | tf_op jit(solution)/shard_map/all_to_all | solution.py:162
  237.5 9.0 %all-to-all-start.3 = ((bf16[32,128,16]{1,2,0:T(8,128)(2,1)}), bf16[32,128,16]{1,2,0:T(8,128)(2,1)S(1)}, u32[]{:S(2)}, u32[]{:S(2)}) async-start(bf16[32,128,16]{1,2,0:T(8,128)(2,1)} %copy.165), calls=%async_computation.3 | async-start | bytes 262144 | tf_op jit(solution)/shard_map/all_to_all | solution.py:151
  249.3 41.7 %psum.7 = f32[]{:T(128)} all-reduce(f32[]{:T(128)} %multiply_reduce_fusion.1), channel_id=1, replica_groups=mesh['ctx'=32,'tp'=16] {'tp'}, use_global_device_ids=true, to_apply=%region_1.2 | all-reduce | flops 1 | bytes 8 | tf_op jit(solution)/shard_map/psum | solution.py:165
  (163 shorter events, 60.2 us)
Async XLA Ops:
  1.7 19.4 %copy-start.3 = (bf16[128,512]{0,1:T(8,128)(2,1)}, bf16[128,512]{0,1:T(8,128)(2,1)S(1)}, u32[]{:S(2)}) copy-start(bf16[128,512]{0,1:T(8,128)(2,1)S(1)} %copy.146) | copy-start | bytes 393220
  2.7 18.8 %copy-start.5 = (bf16[128,512]{0,1:T(8,128)(2,1)}, bf16[128,512]{0,1:T(8,128)(2,1)S(1)}, u32[]{:S(2)}) copy-start(bf16[128,512]{0,1:T(8,128)(2,1)S(1)} %copy.145) | copy-start | bytes 393220
  3.5 84.5 %all-to-all-start = ((bf16[128,32,16]{0,2,1:T(8,128)(2,1)}), bf16[128,32,16]{0,2,1:T(8,128)(2,1)S(1)}, u32[]{:S(2)}, u32[]{:S(2)}) async-start(bf16[128,32,16]{0,2,1:T(8,128)(2,1)} %bitcast.6), calls=%async_computation | async-start | bytes 262144 | tf_op jit(solution)/shard_map/all_to_all | solution.py:128
  20.2 1.4 copy-start.17
  21.1 76.6 %copy-start.15 = (f32[16,16]{1,0:T(8,128)}, f32[16,16]{1,0:T(8,128)S(1)}, u32[]{:S(2)}) copy-start(f32[16,16]{1,0:T(8,128)S(1)} %copy.142) | copy-start | bytes 3076
  23.2 74.1 %copy-start.14 = (f32[16,16]{1,0:T(8,128)}, f32[16,16]{1,0:T(8,128)S(1)}, u32[]{:S(2)}) copy-start(f32[16,16]{1,0:T(8,128)S(1)} %slice_bitcast_fusion) | copy-start | bytes 3076
  88.0 4.1 %copy-start.23 = (f32[16,16]{1,0:T(8,128)}, f32[16,16]{1,0:T(8,128)S(1)}, u32[]{:S(2)}) copy-start(f32[16,16]{1,0:T(8,128)S(1)} %get-tuple-element.73) | copy-start | bytes 3076
  88.0 4.1 %copy-start.22 = (f32[16,16]{1,0:T(8,128)}, f32[16,16]{1,0:T(8,128)S(1)}, u32[]{:S(2)}) copy-start(f32[16,16]{1,0:T(8,128)S(1)} %get-tuple-element.72) | copy-start | bytes 3076
  94.0 3.1 %copy-start.2 = (f32[16,16,32]{1,0,2:T(8,128)S(1)}, f32[16,16,32]{1,0,2:T(8,128)}, u32[]{:S(2)}) copy-start(f32[16,16,32]{1,0,2:T(8,128)} %copy.152) | copy-start | bytes 98308
  97.2 0.7 copy-start.27
  98.0 1.4 copy-start.1
  99.4 15.0 %copy-start.18 = (f32[16,16]{0,1:T(8,128)S(1)}, f32[16,16]{0,1:T(8,128)}, u32[]{:S(2)}) copy-start(f32[16,16]{0,1:T(8,128)} %copy-done.17) | copy-start | bytes 3076
  99.4 15.7 %copy-start.20 = (bf16[128,512]{1,0:T(8,128)(2,1)S(1)}, bf16[128,512]{1,0:T(8,128)(2,1)}, u32[]{:S(2)}) copy-start(bf16[128,512]{1,0:T(8,128)(2,1)} %param.13) | copy-start | bytes 393220
  99.4 15.8 %copy-start.21 = (bf16[128,512]{1,0:T(8,128)(2,1)S(1)}, bf16[128,512]{1,0:T(8,128)(2,1)}, u32[]{:S(2)}) copy-start(bf16[128,512]{1,0:T(8,128)(2,1)} %param.7) | copy-start | bytes 393220
  102.2 20.9 %all-to-all-start.1 = ((bf16[32,128,16]{1,2,0:T(8,128)(2,1)}), bf16[32,128,16]{1,2,0:T(8,128)(2,1)S(1)}, u32[]{:S(2)}, u32[]{:S(2)}) async-start(bf16[32,128,16]{1,2,0:T(8,128)(2,1)} %copy.156), calls=%async_computation.1 | async-start | bytes 262144 | tf_op jit(solution)/shard_map/all_to_all | solution.py:139
  116.0 17.7 %copy-start = (f32[128,16,16]{2,1,0:T(8,128)S(1)}, f32[128,16,16]{2,1,0:T(8,128)}, u32[]{:S(2)}) copy-start(f32[128,16,16]{2,1,0:T(8,128)} %get-tuple-element.70) | copy-start | bytes 393220
  125.0 16.9 %all-to-all-start.2 = ((bf16[128,32,16]{0,2,1:T(8,128)(2,1)}), bf16[128,32,16]{0,2,1:T(8,128)(2,1)S(1)}, u32[]{:S(2)}, u32[]{:S(2)}) async-start(bf16[128,32,16]{0,2,1:T(8,128)(2,1)} %bitcast.12), calls=%async_computation.2 | async-start | bytes 262144 | tf_op jit(solution)/shard_map/all_to_all | solution.py:142
  146.3 0.7 copy-start.7
  146.4 0.7 copy-start.8
  147.1 0.6 copy-start.13
  147.1 1.9 copy-start.12
  182.6 3.4 %copy-start.24 = (f32[1,16,16]{2,1,0:T(8,128)S(1)}, f32[1,16,16]{2,1,0:T(8,128)}, u32[]{:S(2)}) copy-start(f32[1,16,16]{2,1,0:T(8,128)} %slice.494) | copy-start | bytes 3076
  214.5 0.9 copy-start.9
  215.4 1.9 copy-start.19
  215.4 1.9 copy-start.25
  217.3 13.9 %copy-start.10 = (f32[31,16,16]{0,2,1:T(8,128)S(1)}, f32[31,16,16]{0,2,1:T(8,128)}, u32[]{:S(2)}) copy-start(f32[31,16,16]{0,2,1:T(8,128)} %copy.201) | copy-start | bytes 95236
  218.2 19.3 %all-to-all-start.4 = ((f32[32,1,256]{2,1,0:T(1,128)}), f32[32,1,256]{2,1,0:T(1,128)S(1)}, u32[]{:S(2)}, u32[]{:S(2)}) async-start(f32[32,1,256]{2,1,0:T(1,128)} %reshape.133), calls=%async_computation.4 | async-start | bytes 65536 | tf_op jit(solution)/shard_map/all_to_all | solution.py:162
  231.2 17.3 %copy-start.11 = (bf16[128,512]{0,1:T(8,128)(2,1)S(1)}, bf16[128,512]{0,1:T(8,128)(2,1)}, u32[]{:S(2)}) copy-start(bf16[128,512]{0,1:T(8,128)(2,1)} %get-tuple-element.76) | copy-start | bytes 393220
  237.5 55.3 %all-to-all-start.3 = ((bf16[32,128,16]{1,2,0:T(8,128)(2,1)}), bf16[32,128,16]{1,2,0:T(8,128)(2,1)S(1)}, u32[]{:S(2)}, u32[]{:S(2)}) async-start(bf16[32,128,16]{1,2,0:T(8,128)(2,1)} %copy.165), calls=%async_computation.3 | async-start | bytes 262144 | tf_op jit(solution)/shard_map/all_to_all | solution.py:151
  247.7 45.1 %copy-start.4 = (bf16[128,512]{0,1:T(8,128)(2,1)S(1)}, bf16[128,512]{0,1:T(8,128)(2,1)}, u32[]{:S(2)}) copy-start(bf16[128,512]{0,1:T(8,128)(2,1)} %copy-done.3) | copy-start | bytes 393220
  247.7 45.1 %copy-start.6 = (bf16[128,512]{0,1:T(8,128)(2,1)S(1)}, bf16[128,512]{0,1:T(8,128)(2,1)}, u32[]{:S(2)}) copy-start(bf16[128,512]{0,1:T(8,128)(2,1)} %copy-done.5) | copy-start | bytes 393220
  247.8 45.1 %copy-start.26 = (f32[512]{0:T(512)S(1)}, f32[512]{0:T(512)}, u32[]{:S(2)}) copy-start(f32[512]{0:T(512)} %param.12) | copy-start | bytes 6148
  (1 other events, 0.6 us)
